TPU v7x, 1024 devices: a whole 8x8x8 slice. The times are simulated.
1024 devices in a mesh: ep: 64 (over x, y), tp: 16 (over z, core).
Axes of the slice: x: 8, y: 8, z: 8, core: 2. Of those that a mesh axis runs over, the one named last changes fastest.
Arguments:
- tokens: bfloat16 [2048, 4096], P('ep', 'tp'), may hold values from -6 to 6
- grad_out: bfloat16 [2048, 4096], P('ep', 'tp'), may hold values from -6 to 6
- combine: bfloat16 [2048, 8], P('ep'), may hold values from 0.049804688 to 0.5
- expert_ids: int32 [2048, 8], P('ep'), may hold values from 0 to 63, all different within a row; in each aligned block of 32 rows (0 to 31, 32 to 63, ...) at most 5 rows name the same one
- w_gate: bfloat16 [64, 4096, 1536], P('ep', None, 'tp'), may hold values from -0.09375 to 0.09375
- w_up: bfloat16 [64, 4096, 1536], P('ep', None, 'tp'), may hold values from -0.09375 to 0.09375
- w_down: bfloat16 [64, 1536, 4096], P('ep', 'tp'), may hold values from -0.15625 to 0.15625
Outputs:
- d_tokens: bfloat16 [2048, 4096], P('ep', 'tp')
- d_combine: float32 [2048, 8], P('ep')
- grad_down: bfloat16 [64, 1536, 4096], P('ep', 'tp')
Inputs may be any that keep to these rules, and one draw needn't show every extreme that they name: `expert_ids`: among the 32 tokens of one index of ep, no expert is named by more than 5 assignments, and some expert reaches 5; a token names 8 different experts.
All inputs are finite; a program needn't handle non-finite values.
Results may differ from a plain program's by a relative error of at most 0.025.
Values may be sent and summed in bfloat16 or wider, within the bound.
A program may use at most 32 MiB of HBM per device.

v0:
```python
import jax
import jax.numpy as jnp
from jax import lax
from jax.sharding import PartitionSpec as P


def per_device(tokens, grad_out, combine, expert_ids, w_gate, w_up, w_down):
    tok_count, feat_local = tokens.shape
    top_count = expert_ids.shape[1]
    expert_count = lax.axis_size("ep")
    tp_count = lax.axis_size("tp")
    capacity = tok_count * top_count * 5 // (4 * expert_count)
    slot_total = expert_count * capacity
    contract_first = (((0,), (0,)), ((), ()))
    contract_last = (((1,), (1,)), ((), ()))
    flat_ids = expert_ids.reshape(-1)
    expert_hot = (flat_ids[:, None] == lax.iota(jnp.int32, expert_count)[None, :]).astype(jnp.int32)
    slot_index = jnp.sum((jnp.cumsum(expert_hot, axis=0) - expert_hot) * expert_hot, axis=1)
    position = flat_ids * capacity + slot_index
    placement = (position[:, None] == lax.iota(jnp.int32, slot_total)[None, :]).astype(jnp.float32)
    token_slot = jnp.sum(placement.reshape(tok_count, top_count, slot_total), axis=1).astype(
        jnp.bfloat16
    )
    x_slots = lax.dot_general(
        token_slot, tokens, contract_first, preferred_element_type=jnp.float32
    ).astype(jnp.bfloat16)
    dy_slots = lax.dot_general(
        token_slot, grad_out, contract_first, preferred_element_type=jnp.float32
    ).astype(jnp.bfloat16)
    w_slots = jnp.sum(placement * combine.reshape(-1, 1).astype(jnp.float32), axis=0).astype(
        jnp.bfloat16
    )
    x_recv, dy_recv, w_recv = (
        lax.all_to_all(
            x_slots.reshape(expert_count, capacity, feat_local),
            "ep",
            split_axis=0,
            concat_axis=0,
            tiled=True,
        ),
        lax.all_to_all(
            dy_slots.reshape(expert_count, capacity, feat_local),
            "ep",
            split_axis=0,
            concat_axis=0,
            tiled=True,
        ),
        lax.all_to_all(
            w_slots.reshape(expert_count, capacity), "ep", split_axis=0, concat_axis=0, tiled=True
        ),
    )
    down_matrix = w_down[0]
    hidden_local = w_gate.shape[2]
    paired = jnp.concatenate([w_gate[0], w_up[0]], axis=1)
    full_x, full_dy = (
        lax.all_gather(x_recv, "tp", axis=2, tiled=True),
        lax.all_gather(dy_recv, "tp", axis=2, tiled=True),
    )
    full_x = full_x.reshape(slot_total, -1)
    full_dy = full_dy.reshape(slot_total, -1)
    both_pre = jnp.dot(full_x, paired, preferred_element_type=jnp.float32)
    hidden_grad = lax.dot_general(
        full_dy, down_matrix, contract_last, preferred_element_type=jnp.float32
    )
    gate_pre = both_pre[:, :hidden_local]
    up_pre = both_pre[:, hidden_local:]
    weight_col = w_recv.reshape(slot_total, 1).astype(jnp.float32)
    activation = jax.nn.silu(gate_pre)
    product = activation * up_pre
    hidden = product.astype(jnp.bfloat16)
    weighted = (weight_col * product).astype(jnp.bfloat16)
    comb_part = jnp.sum(hidden.astype(jnp.float32) * hidden_grad, axis=1)
    scaled = weight_col * hidden_grad
    up_grad = (scaled * activation).astype(jnp.bfloat16)
    sigma = jax.nn.sigmoid(gate_pre)
    gate_grad = (scaled * up_pre * sigma * (1.0 + gate_pre * (1.0 - sigma))).astype(jnp.bfloat16)
    both_grad = jnp.concatenate([gate_grad, up_grad], axis=1)
    input_part = lax.dot_general(
        both_grad, paired, contract_last, preferred_element_type=jnp.float32
    )
    comb_spread = jnp.broadcast_to(
        comb_part.reshape(expert_count, capacity, 1), (expert_count, capacity, tp_count)
    )
    input_sum, comb_sum = (
        lax.psum_scatter(
            input_part.reshape(expert_count, capacity, -1).astype(jnp.bfloat16),
            "tp",
            scatter_dimension=2,
            tiled=True,
        ).astype(jnp.float32),
        lax.psum_scatter(
            comb_spread.astype(jnp.bfloat16), "tp", scatter_dimension=2, tiled=True
        ).astype(jnp.float32),
    )
    down_grad = lax.dot_general(
        weighted, full_dy, contract_first, preferred_element_type=jnp.float32
    )
    rounded = lax.optimization_barrier(input_sum.astype(jnp.bfloat16)).astype(jnp.float32)
    back_input, back_comb = (
        lax.all_to_all(
            rounded.astype(jnp.bfloat16), "ep", split_axis=0, concat_axis=0, tiled=True
        ).astype(rounded.dtype),
        lax.all_to_all(
            comb_sum.astype(jnp.bfloat16), "ep", split_axis=0, concat_axis=0, tiled=True
        ).astype(comb_sum.dtype),
    )
    back_rows = back_input.reshape(slot_total, feat_local).astype(jnp.bfloat16)
    d_tokens = jnp.dot(token_slot, back_rows, preferred_element_type=jnp.float32).astype(
        jnp.bfloat16
    )
    d_combine = jnp.dot(
        placement, back_comb.reshape(slot_total, 1), precision=lax.Precision.HIGHEST
    )
    return (d_tokens, d_combine.reshape(tok_count, top_count), down_grad.astype(jnp.bfloat16)[None])


def solution(mesh):
    placed = (
        P("ep", "tp"),
        P("ep", "tp"),
        P("ep", None),
        P("ep", None),
        P("ep", None, "tp"),
        P("ep", None, "tp"),
        P("ep", "tp", None),
    )
    return jax.shard_map(
        per_device,
        mesh=mesh,
        in_specs=placed,
        out_specs=(P("ep", "tp"), P("ep", None), P("ep", "tp", None)),
        check_vma=False,
    )
```

profile of v0, /device:TPU:1, one launch (start us, length us, event | category | flops | bytes accessed | tf_op | source)
XLA Modules:
  0.0 263.1 jit_solution(7567370569965966295)
XLA Ops:
  7.2 0.0 copy-start
  7.2 0.0 copy-start.5
  7.2 0.0 all-gather.5.cloned.1.call-start
  7.2 0.8 copy.31
  8.1 0.1 eq.67
  8.1 0.1 eq.71
  8.3 0.6 reduce-window.6
  8.9 0.2 slice_reduce_fusion
  9.1 0.1 fusion.15
  9.2 0.1 reduce_sum.39
  9.3 0.2 convert_reduce_fusion
  9.5 0.9 convolution_convert_fusion.2
  10.5 0.1 reshape.131
  10.5 26.4 %all_to_all.26 = bf16[64,5,256]{2,1,0:T(8,128)(2,1)} all-to-all(bf16[64,5,256]{2,1,0:T(8,128)(2,1)S(1)} %reshape.131), channel_id=1, replica_groups=mesh['ep'=64,'tp'=16] {'ep'}, dimensions={0} | all-to-all | bytes 327680 | tf_op jit(solution)/shard_map/all_to_all | solution.py:34
  37.0 0.0 all-gather.5.cloned.1.call-update
  37.0 0.0 all-gather.3.cloned.1.call-start
  37.0 0.9 convolution_convert_fusion.3
  38.0 0.1 reshape.129
  38.1 17.0 %all_to_all.27 = bf16[64,5,256]{2,1,0:T(8,128)(2,1)} all-to-all(bf16[64,5,256]{2,1,0:T(8,128)(2,1)S(1)} %reshape.129), channel_id=1, replica_groups=mesh['ep'=64,'tp'=16] {'ep'}, dimensions={0} | all-to-all | bytes 327680 | tf_op jit(solution)/shard_map/all_to_all | solution.py:41
  55.1 0.0 all-gather.3.cloned.1.call-update
  55.1 0.0 reduce-scatter.2.cloned.1.call-start
  55.2 0.0 copy-done.5
  55.2 0.1 copy.35
  55.2 0.1 reshape.134
  55.4 0.1 select_reduce_fusion
  55.5 0.2 convert_element_type.128
  55.7 14.6 %all_to_all.28 = bf16[64,1,5]{2,1,0:T(2,128)(2,1)S(1)} all-to-all(bf16[64,1,5]{2,1,0:T(2,128)(2,1)S(1)} %convert_element_type.128), channel_id=1, replica_groups=mesh['ep'=64,'tp'=16] {'ep'}, dimensions={0} | all-to-all | bytes 1280 | tf_op jit(solution)/shard_map/all_to_all | solution.py:48
  70.3 0.1 convert_reduce_fusion.1
  70.4 0.1 reshape.135
  70.5 26.9 %all-gather.5.cloned.1.call-done = bf16[64,5,4096]{2,1,0:T(8,128)(2,1)} async-done(((bf16[64,5,256]{2,1,0:T(8,128)(2,1)}), bf16[64,5,4096]{2,1,0:T(8,128)(2,1)}) %all-gather.5.cloned.1.call-update) | async-done | bytes 2621456 | tf_op jit(solution)/shard_map/all_gather | solution.py:56
  97.4 3.4 %reshape.132 = bf16[320,4096]{1,0:T(8,128)(2,1)S(1)} reshape(bf16[64,5,4096]{2,1,0:T(8,128)(2,1)} %all-gather.5.cloned.1.call-done) | data formatting | bytes 5242880 | tf_op jit(solution)/shard_map/reshape | solution.py:59
  100.8 3.3 %fusion.1 = f32[320,192]{0,1:T(8,128)} fusion(bf16[320,4096]{1,0:T(8,128)(2,1)S(1)} %reshape.132, bf16[4096,96]{0,1:T(8,128)(2,1)} %bitcast.43, bf16[4096,96]{0,1:T(8,128)(2,1)} %bitcast.45), kind=kOutput, calls=%fused_computation.7 | convolution fusion | flops 506462208 | bytes 4440064 | tf_op jit(solution)/shard_map/dot_general | solution.py:61
  104.1 50.1 %all-gather.3.cloned.1.call-done = bf16[64,5,4096]{2,1,0:T(8,128)(2,1)} async-done(((bf16[64,5,256]{2,1,0:T(8,128)(2,1)}), bf16[64,5,4096]{2,1,0:T(8,128)(2,1)}) %all-gather.3.cloned.1.call-update) | async-done | bytes 2621456 | tf_op jit(solution)/shard_map/all_gather | solution.py:57
  154.2 3.4 %reshape.130 = bf16[320,4096]{1,0:T(8,128)(2,1)S(1)} reshape(bf16[64,5,4096]{2,1,0:T(8,128)(2,1)} %all-gather.3.cloned.1.call-done) | data formatting | bytes 5242880 | tf_op jit(solution)/shard_map/reshape | solution.py:60
  157.6 0.0 copy-done
  157.7 0.0 copy-start.1
  157.7 0.0 copy-start.3
  157.7 0.0 copy-start.4
  157.7 2.5 multiply_convert_fusion.2
  160.1 0.0 copy-done.1
  160.2 0.0 copy-done.3
  160.2 0.0 copy-done.4
  160.2 0.9 convolution_convert_fusion
  161.1 2.9 %convert_element_type.117 = bf16[64,5,4096]{2,1,0:T(8,128)(2,1)} reshape(bf16[320,4096]{1,0:T(8,128)(2,1)S(1)} %convolution_convert_fusion) | data formatting | bytes 5242880 | tf_op jit(solution)/shard_map/convert_element_type | solution.py:86
  163.9 0.0 reduce-scatter.2.cloned.1.call-update
  164.0 1.4 dynamic-slice
  165.4 0.1 convert_element_type.123
  165.5 0.1 copy.37
  165.6 45.4 %all-reduce = bf16[64,5,16]{0,1,2:T(8,128)(2,1)S(1)} all-reduce(bf16[64,5,16]{0,1,2:T(8,128)(2,1)S(1)} %broadcast_in_dim.4), channel_id=3, replica_groups=mesh['ep'=64,'tp'=16] {'tp'}, use_global_device_ids=true, to_apply=%region_7.8.clone | all-reduce | flops 5120 | bytes 20480
  211.0 0.6 constant_dynamic-slice_fusion
  211.7 0.7 copy.38
  212.4 12.4 %all-to-all-start.4 = ((bf16[64,5,1]{1,2,0:T(2,128)(2,1)}), bf16[64,5,1]{1,2,0:T(2,128)(2,1)S(1)}, u32[]{:S(2)}, u32[]{:S(2)}) async-start(bf16[64,5,1]{1,2,0:T(2,128)(2,1)} %copy.38), calls=%async_computation.5 | async-start | bytes 65536 | tf_op jit(solution)/shard_map/all_to_all | solution.py:103
  224.8 5.2 %reduce-scatter.2.cloned.1.call-done = bf16[64,5,256]{2,1,0:T(8,128)(2,1)} async-done(((bf16[64,5,4096]{2,1,0:T(8,128)(2,1)}), bf16[64,5,256]{2,1,0:T(8,128)(2,1)}) %reduce-scatter.2.cloned.1.call-update) | async-done | bytes 163856 | tf_op jit(solution)/shard_map/reduce_scatter | solution.py:85
  230.0 5.6 %all-to-all-done.4 = bf16[64,5,1]{1,2,0:T(2,128)(2,1)S(1)} async-done(((bf16[64,5,1]{1,2,0:T(2,128)(2,1)}), bf16[64,5,1]{1,2,0:T(2,128)(2,1)S(1)}, u32[]{:S(2)}, u32[]{:S(2)}) %all-to-all-start.4) | async-done | bytes 672 | tf_op jit(solution)/shard_map/all_to_all | solution.py:103
  235.5 6.9 %all-to-all-start.3 = ((bf16[64,5,256]{2,1,0:T(8,128)(2,1)}), bf16[64,5,256]{2,1,0:T(8,128)(2,1)}, u32[]{:S(2)}, u32[]{:S(2)}) async-start(bf16[64,5,256]{2,1,0:T(8,128)(2,1)} %reduce-scatter.2.cloned.1.call-done), calls=%async_computation.4 | async-start | bytes 524288 | tf_op jit(solution)/shard_map/all_to_all | solution.py:100
  242.4 0.0 copy-done.2
  242.4 2.6 fusion
  245.0 0.1 reduce.2
  245.1 0.1 reshape.136
  245.3 0.8 fusion.5
  246.0 0.7 copy.39
  246.7 8.1 %all-to-all-done.3 = bf16[64,5,256]{2,1,0:T(8,128)(2,1)} async-done(((bf16[64,5,256]{2,1,0:T(8,128)(2,1)}), bf16[64,5,256]{2,1,0:T(8,128)(2,1)}, u32[]{:S(2)}, u32[]{:S(2)}) %all-to-all-start.3) | async-done | bytes 163872 | tf_op jit(solution)/shard_map/all_to_all | solution.py:100
  254.8 1.0 convert_element_type.118
  255.8 0.8 convolution_convert_fusion.4
  (7 shorter events, 0.1 us)
Async XLA Ops:
  7.2 150.5 %copy-start = (bf16[1,96,4096]{2,1,0:T(8,128)(2,1)S(1)}, bf16[1,96,4096]{2,1,0:T(8,128)(2,1)}, u32[]{:S(2)}) copy-start(bf16[1,96,4096]{2,1,0:T(8,128)(2,1)} %param.13) | copy-start | bytes 2359300
  7.2 48.0 %copy-start.5 = (bf16[32,8]{0,1:T(8,128)(2,1)S(1)}, bf16[32,8]{0,1:T(8,128)(2,1)}, u32[]{:S(2)}) copy-start(bf16[32,8]{0,1:T(8,128)(2,1)} %param.9) | copy-start | bytes 1540
  7.2 90.2 %all-gather.5.cloned.1.call-start = ((), (), s32[]{:S(2)}) async-start(), calls=%async_computation.7 | async-start | bytes 4456448 | tf_op jit(solution)/shard_map/all_gather | solution.py:56
  37.0 117.2 %all-gather.3.cloned.1.call-start = ((), (), s32[]{:S(2)}) async-start(), calls=%async_computation.6 | async-start | bytes 4456448 | tf_op jit(solution)/shard_map/all_gather | solution.py:57
  55.1 174.9 %reduce-scatter.2.cloned.1.call-start = ((), (), s32[]{:S(2)}) async-start(), calls=%async_computation.8 | async-start | bytes 4456448 | tf_op jit(solution)/shard_map/reduce_scatter | solution.py:85
  157.7 2.5 copy-start.1
  157.7 2.5 copy-start.3
  157.7 2.5 copy-start.4
  163.9 78.5 %copy-start.2 = (bf16[320,4096]{1,0:T(8,128)(2,1)S(1)}, bf16[320,4096]{1,0:T(8,128)(2,1)}, u32[]{:S(2)}) copy-start(bf16[320,4096]{1,0:T(8,128)(2,1)} %copy-done.1) | copy-start | bytes 7864324
  212.4 23.2 %all-to-all-start.4 = ((bf16[64,5,1]{1,2,0:T(2,128)(2,1)}), bf16[64,5,1]{1,2,0:T(2,128)(2,1)S(1)}, u32[]{:S(2)}, u32[]{:S(2)}) async-start(bf16[64,5,1]{1,2,0:T(2,128)(2,1)} %copy.38), calls=%async_computation.5 | async-start | bytes 65536 | tf_op jit(solution)/shard_map/all_to_all | solution.py:103
  235.5 19.3 %all-to-all-start.3 = ((bf16[64,5,256]{2,1,0:T(8,128)(2,1)}), bf16[64,5,256]{2,1,0:T(8,128)(2,1)}, u32[]{:S(2)}, u32[]{:S(2)}) async-start(bf16[64,5,256]{2,1,0:T(8,128)(2,1)} %reduce-scatter.2.cloned.1.call-done), calls=%async_computation.4 | async-start | bytes 524288 | tf_op jit(solution)/shard_map/all_to_all | solution.py:100
Sparse Core Ops, SparseCore 0:
  37.1 60.2 all-gather.4
  100.0 54.1 all-gather.2
  164.1 65.8 reduce-scatter.1
where the time goes:
time: 266 us; the launch traced here: 263 us
  blocking collectives  103 us (39%)
  waiting for transfers between devices  95.9 us (36%)
  starting transfers between devices  19.4 us (7%)
  local copies, waits for them, and re-layouts  16.5 us (6%)
  between operations  14 us (5%)
  matrix products  12.6 us (5%)
    all_gather x1, waiting for transfers between devices, per_device(): lax.all_gather(dy_recv, 'tp', axis=2, tiled=True)  50.1 us
    unnamed x1, blocking collectives  45.4 us
    all_gather x1, waiting for transfers between devices, per_device(): lax.all_gather(x_recv, 'tp', axis=2, tiled=True)  26.9 us
    all_to_all x1, blocking collectives, per_device(): lax.all_to_all(x_slots.reshape(expert_count, capacity, feat_local), 'ep',...  26.4 us
    all_to_all x1, blocking collectives, per_device(): lax.all_to_all(dy_slots.reshape(expert_count, capacity, feat_local), 'ep'...  17 us
    all_to_all x1, blocking collectives, per_device(): lax.all_to_all(w_slots.reshape(expert_count, capacity), 'ep', split_axis=...  14.6 us
    all_to_all x1, starting transfers between devices, per_device(): lax.all_to_all(comb_sum.astype(jnp.bfloat16), 'ep', split_axis=0, concat_...  12.4 us
    all_to_all x1, waiting for transfers between devices, per_device(): lax.all_to_all(rounded.astype(jnp.bfloat16), 'ep', split_axis=0, concat_a...  8.11 us
  transfers between devices with their start and end apart: 5, of which 5 were waited for; matrix products, arithmetic and copies ran while one was open for 6% of the time, Pallas kernels for 0%

commit v1 on v0

v1 whole, which is shorter than its diff:
```python
import functools

import jax
import jax.numpy as jnp
from jax import lax
from jax.experimental import pallas as pl
from jax.experimental.pallas import tpu as pltpu
from jax.sharding import PartitionSpec as P

MESH = pl.DeviceIdType.MESH
F32 = jnp.float32
BF16 = jnp.bfloat16
CAP = 5
GROUP = 16
NN = (((1,), (0,)), ((), ()))
NT = (((1,), (1,)), ((), ()))
TN = (((0,), (0,)), ((), ()))


def dot(a, b, dims=NN, precision=None):
    return lax.dot_general(a, b, dims, preferred_element_type=F32, precision=precision)


def iota(shape, dim):
    return lax.broadcasted_iota(jnp.int32, shape, dim)


def packed_row(i):
    part = (i >= 80).astype(jnp.int32) + (i >= 160).astype(jnp.int32)
    j = i - part * 80
    s = (j * 205) >> 10
    c = j - s * 5
    scalar = s * 16 + c + 5 + jnp.where(c >= 3, 5, 0)
    return jnp.where(part == 2, scalar, s * 16 + part * 8 + c)


def kernel(
    n_ep,
    n_tp,
    ids,
    comb,
    tok,
    gout,
    wg,
    wu,
    wd,
    dtok,
    dcomb,
    gdown,
    w2,
    wdp,
    ohx,
    ohw,
    sx,
    sdy,
    rx,
    rdy,
    fx,
    fdy,
    acc,
    acch,
    wcol,
    bg,
    wt,
    cb,
    pown,
    pout,
    pin,
    sbuf,
    arr_r,
    arr_l,
    sback,
    rback,
    gd,
    w_sem,
    ep_s,
    ep_r,
    ag_rs,
    ag_rr,
    ag_ls,
    ag_lr,
    sib_s,
    sib_r,
    pair_s,
    pair_r,
    rs_rs,
    rs_rr,
    rs_ls,
    rs_lr,
    cb_s,
    cb_r,
    gd_sem,
):
    nz = n_tp // 2
    ep = lax.axis_index("ep")
    tp = lax.axis_index("tp")
    z = lax.div(tp, 2)
    c = lax.rem(tp, 2)
    right = lax.rem(z + 1, nz) * 2 + c
    left = lax.rem(z + nz - 1, nz) * 2 + c
    sib = z * 2 + 1 - c
    slots = fx.shape[1]
    feat = fx.shape[2]
    half_rows = slots // 2
    hid = wg.shape[0]
    groups = n_ep // GROUP

    def rcopy(src, dst, s, r, axis, to):
        return pltpu.make_async_remote_copy(
            src_ref=src, dst_ref=dst, send_sem=s, recv_sem=r, device_id={axis: to}, device_id_type=MESH
        )

    loads = (
        pltpu.make_async_copy(wg, w2.at[pl.ds(0, hid)], w_sem.at[0]),
        pltpu.make_async_copy(wu, w2.at[pl.ds(128, hid)], w_sem.at[1]),
        pltpu.make_async_copy(wd, wdp.at[pl.ds(0, hid)], w_sem.at[2]),
    )
    for load in loads:
        load.start()

    barrier = pltpu.get_barrier_semaphore()

    def greet_ep(i, _):
        pl.semaphore_signal(barrier, inc=1, device_id={"ep": lax.rem(ep + i, n_ep)}, device_id_type=MESH)
        return 0

    def greet_tp(i, _):
        pl.semaphore_signal(barrier, inc=1, device_id={"tp": lax.rem(tp + i, n_tp)}, device_id_type=MESH)
        return 0

    lax.fori_loop(1, n_ep, greet_ep, 0)
    lax.fori_loop(1, n_tp, greet_tp, 0)

    tokens = tok.shape[0]
    expert = iota((n_ep, tokens), 0)
    named = jnp.zeros((n_ep, tokens), F32)
    weight = jnp.zeros((n_ep, tokens), F32)
    for k in range(ids.shape[0]):
        hit = ids[k : k + 1, :] == expert
        named = jnp.where(hit, 1.0, named)
        weight = jnp.where(hit, comb[k : k + 1, :].astype(F32), weight)
    earlier = (iota((tokens, tokens), 0) < iota((tokens, tokens), 1)).astype(F32).astype(BF16)
    rank = dot(named.astype(BF16), earlier)
    code = jnp.where(named > 0.5, rank, 99.0).astype(BF16)
    weight = weight.astype(BF16)
    for g in range(groups):
        row = iota((256, n_ep), 0) + 256 * g
        spread = ((row >> 4) == iota((256, n_ep), 1)).astype(F32).astype(BF16)
        code_rows = dot(spread, code)
        weight_rows = dot(spread, weight)
        r = iota((256, tokens), 0)
        cc = r & 7
        wanted = jnp.where(cc < CAP, cc, cc - CAP + 3 * ((r >> 3) & 1)).astype(F32)
        hot = (code_rows == wanted).astype(F32)
        rows = pl.ds(256 * g, 256)
        ohx[rows, :] = jnp.where(cc < CAP, hot, 0.0).astype(BF16)
        ohw[rows, :] = jnp.where(cc < CAP, 0.0, hot).astype(BF16)
        scalar = dot((jnp.where(cc < CAP, 0.0, hot) * weight_rows).astype(BF16), jnp.ones((tokens, 128), BF16))
        both = dot(ohx[rows, :], tok[...])
        upper = (iota((256, 128), 0) & 8) == 0
        block = jnp.where(upper, both[:, :128], both[:, 128:]) + scalar
        sx[pl.ds(GROUP * g, GROUP)] = block.astype(BF16).reshape(GROUP, 16, 128)

    pl.semaphore_wait(barrier, n_ep - 1 + n_tp - 1)

    def send_blocks(src, dst, index):
        def one(i, _):
            to = lax.rem(ep + i, n_ep)
            rcopy(src.at[to], dst.at[ep], ep_s.at[index], ep_r.at[index], "ep", to).start()
            return 0

        lax.fori_loop(1, n_ep, one, 0)
        dst[pl.ds(ep, 1)] = src[pl.ds(ep, 1)]

    def all_blocks(src, dst, index):
        some = pl.ds(0, n_ep - 1)
        return rcopy(src.at[some], dst.at[some], ep_s.at[index], ep_r.at[index], "ep", lax.rem(ep + 1, n_ep))

    send_blocks(sx, rx, 0)
    for g in range(groups):
        rows = pl.ds(256 * g, 256)
        both = dot(ohx[rows, :], gout[...])
        upper = (iota((256, 128), 0) & 8) == 0
        block = jnp.where(upper, both[:, :128], both[:, 128:])
        sdy[pl.ds(GROUP * g, GROUP)] = block.astype(BF16).reshape(GROUP, 16, 128)
    send_blocks(sdy, rdy, 1)

    gap = 128 - hid
    blank = jnp.zeros((gap, w2.shape[1]), BF16)
    w2[pl.ds(hid, gap), :] = blank
    w2[pl.ds(128 + hid, gap), :] = blank
    wdp[pl.ds(hid, gap), :] = blank
    acc[...] = jnp.zeros_like(acc)
    acch[...] = jnp.zeros_like(acch)
    cb[pl.ds(tp, 1)] = jnp.zeros((1, 8, 128), F32)
    for load in loads:
        load.wait()
    pick = (iota((240, 256), 1) == packed_row(iota((240, 256), 0))).astype(F32).astype(BF16)

    full = (fx, fdy)
    got = (rx, rdy)
    sent = (sx, sdy)

    def half(ref, h):
        return ref.at[pl.ds(h * half_rows, half_rows)]

    def chunk(k, own):
        return lax.rem(z + k + nz, nz) * 2 + (c if own else 1 - c)

    def to_right(t, j, h, q):
        piece = half(full[t].at[q], h)
        return rcopy(piece, piece, ag_rs.at[t, j, h], ag_rr.at[t, j, h], "tp", right)

    def to_left(t, j, h, q):
        piece = half(full[t].at[q], h)
        return rcopy(piece, piece, ag_ls.at[t, j, h], ag_lr.at[t, j, h], "tp", left)

    def to_sib(t, i, q):
        piece = full[t].at[q]
        return rcopy(piece, piece, sib_s.at[t, i], sib_r.at[t, i], "tp", sib)

    def consume(t, q):
        columns = pl.ds(pl.multiple_of(q * feat, feat), feat)
        if t == 0:
            acc[...] += dot(fx[q], w2[:, columns], NT)
        else:
            acch[...] += dot(fdy[q], wdp[:, columns], NT)

    def consume_pair(t, j, own):
        def one(i, _):
            consume(t, chunk(j * (2 * i - 1), own))
            return 0

        lax.fori_loop(0, 2, one, 0)

    mine = chunk(0, True)
    for t in range(2):
        all_blocks(sent[t], got[t], t).wait_recv()
        for g in range(groups):
            block = got[t][pl.ds(GROUP * g, GROUP)].reshape(256, 128)
            packed = dot(pick if t == 0 else pick[:160], block)
            rows = pl.ds(80 * g, 80)
            full[t][tp, rows, :128] = packed[:80].astype(BF16)
            full[t][tp, rows, 128:] = packed[80:160].astype(BF16)
            if t == 0:
                wcol[rows, :] = packed[160:]
        to_right(t, 0, 0, mine).start()
        to_left(t, 0, 1, mine).start()
        to_right(t, 0, 1, mine).start()
        to_left(t, 0, 0, mine).start()
        to_sib(t, 0, mine).start()
    consume(0, mine)
    consume(1, mine)
    for t in range(2):
        to_sib(t, 0, chunk(0, False)).wait_recv()
        consume(t, chunk(0, False))

    def stage(j, _):
        for t in range(2):
            from_left, from_right = chunk(-j, True), chunk(j, True)
            to_right(t, j - 1, 0, from_left).wait_recv()
            to_right(t, j, 0, from_left).start()
            to_left(t, j - 1, 1, from_right).wait_recv()
            to_left(t, j, 1, from_right).start()
            to_right(t, j - 1, 1, from_left).wait_recv()

            @pl.when(j < nz // 2 - 1)
            def _():
                to_right(t, j, 1, from_left).start()

            to_left(t, j - 1, 0, from_right).wait_recv()

            @pl.when(j < nz // 2 - 1)
            def _():
                to_left(t, j, 0, from_right).start()

            to_sib(t, j, from_left).start()
            to_sib(t, nz // 2 + j, from_right).start()
            consume_pair(t, j, True)
        for t in range(2):
            to_sib(t, j, chunk(-j, False)).wait_recv()
            to_sib(t, nz // 2 + j, chunk(j, False)).wait_recv()
            consume_pair(t, j, False)
        return 0

    last = nz // 2
    lax.fori_loop(1, last, stage, 0)
    for t in range(2):
        q = chunk(last, True)
        to_right(t, last - 1, 0, q).wait_recv()
        to_left(t, last - 1, 1, q).wait_recv()
        to_sib(t, last, q).start()
        consume(t, q)
    for t in range(2):
        q = chunk(last, False)
        to_sib(t, last, q).wait_recv()
        consume(t, q)

    for g in range(groups):
        rows = pl.ds(80 * g, 80)
        gate, up, back = acc[rows, :128], acc[rows, 128:], acch[rows, :]
        w = wcol[rows, :]
        sigma = jax.nn.sigmoid(gate)
        act = gate * sigma
        product = act * up
        hidden = product.astype(BF16).astype(F32)
        wt[rows, :] = (w * product).astype(BF16)
        scaled = w * back
        bg[rows, :128] = (scaled * up * sigma * (1.0 + gate * (1.0 - sigma))).astype(BF16)
        bg[rows, 128:] = (scaled * act).astype(BF16)
        line = dot(jnp.ones((8, 128), F32), hidden * back, NT, lax.Precision.HIGHEST)
        cb[tp, g : g + 1, :80] = line[:1]

    def pair(k):
        return rcopy(pout.at[k], pin.at[k], pair_s.at[k], pair_r.at[k], "tp", sib)

    def calc(k):
        def part(q):
            columns = pl.ds(pl.multiple_of(q * feat, feat), feat)
            return dot(bg[...], w2[:, columns]).astype(BF16)

        pout[k] = part(chunk(k, False))
        pair(k).start()
        pown[k] = part(chunk(k, True))

    def calc_pair(k):
        def one(i, _):
            calc(k + i * (nz - 2 * k))
            return 0

        lax.fori_loop(0, 2, one, 0)

    def put(k, h, arrived):
        rows = pl.ds(h * half_rows, half_rows)
        value = pown[k, rows, :].astype(F32) + pin[k, rows, :].astype(F32)
        if arrived is not None:
            value = value + arrived[rows, :].astype(F32)
        sbuf[k, rows, :] = value.astype(BF16)

    def sum_right(k, h):
        return rcopy(
            half(sbuf.at[k], h), half(arr_r.at[k - 1], h), rs_rs.at[k - 1, h], rs_rr.at[k - 1, h], "tp", right
        )

    def sum_left(k, h):
        return rcopy(
            half(sbuf.at[nz - k], h), half(arr_l.at[k - 1], h), rs_ls.at[k - 1, h], rs_lr.at[k - 1, h], "tp", left
        )

    calc(last)
    calc_pair(last - 1)

    def tell(i, _):
        rcopy(cb.at[tp], cb.at[tp], cb_s, cb_r, "tp", lax.rem(tp + i, n_tp)).start()
        return 0

    lax.fori_loop(1, n_tp, tell, 0)
    pair(last).wait_recv()
    put(last, 0, None)
    sum_right(last, 0).start()
    put(last, 1, None)
    sum_left(last, 1).start()
    for k in range(last - 1, 0, -1):
        first = k == last - 1
        pair(k).wait_recv()
        if not first:
            sum_right(k + 1, 1).wait_recv()
        put(k, 1, None if first else arr_r.at[k])
        sum_right(k, 1).start()
        pair(nz - k).wait_recv()
        if not first:
            sum_left(k + 1, 0).wait_recv()
        put(nz - k, 0, None if first else arr_l.at[k])
        sum_left(k, 0).start()
        if k > 1:
            calc_pair(k - 1)
        else:
            calc(0)
        sum_right(k + 1, 0).wait_recv()
        put(k, 0, arr_r.at[k])
        sum_right(k, 0).start()
        sum_left(k + 1, 1).wait_recv()
        put(nz - k, 1, arr_l.at[k])
        sum_left(k, 1).start()

    some = pl.ds(0, n_tp - 1)
    comb_all = rcopy(cb.at[some], cb.at[some], cb_s, cb_r, "tp", right)
    comb_all.wait_recv()
    comb_sum = jnp.sum(cb[...], axis=0)
    place = (iota((256, 160), 0) == packed_row(iota((256, 160), 1))).astype(F32).astype(BF16)
    place_scalar = (iota((256, 80), 0) == packed_row(iota((256, 80), 1) + 160)).astype(F32)
    pair(0).wait_recv()
    for h in (1, 0):
        sum_right(1, h).wait_recv()
        sum_left(1, h).wait_recv()
    for g in range(groups):
        rows = pl.ds(80 * g, 80)
        total = pown[0, rows, :].astype(F32) + pin[0, rows, :].astype(F32)
        total = total + arr_r[0, rows, :].astype(F32) + arr_l[0, rows, :].astype(F32)
        total = total.astype(BF16)
        packed = jnp.concatenate([total[:, :128], total[:, 128:]], axis=0)
        line = (place_scalar * comb_sum[g : g + 1, :80]).astype(BF16)
        block = dot(place, packed) + dot(line, jnp.ones((80, 128), BF16))
        sback[pl.ds(GROUP * g, GROUP)] = block.astype(BF16).reshape(GROUP, 16, 128)
    send_blocks(sback, rback, 2)

    def down(q, _):
        columns = pl.ds(pl.multiple_of(q * feat, feat), feat)
        gd[:, columns] = dot(wt[...], fdy[q], TN)[:hid].astype(BF16)
        return 0

    lax.fori_loop(0, n_tp, down, 0)
    out = pltpu.make_async_copy(gd, gdown, gd_sem)
    out.start()

    all_blocks(sback, rback, 2).wait_recv()
    back = rback[...].reshape(n_ep * 16, 128)
    hot = ohx[...]
    upper = (iota((n_ep * 16, tokens), 0) & 8) == 0
    zero = jnp.zeros_like(hot)
    dtok[:, :128] = dot(jnp.where(upper, hot, zero), back, TN).astype(BF16)
    dtok[:, 128:] = dot(jnp.where(upper, zero, hot), back, TN).astype(BF16)
    chosen = ohw[...] * back[:, :tokens]
    gather = ((iota((n_ep, n_ep * 16), 1) >> 4) == iota((n_ep, n_ep * 16), 0)).astype(F32).astype(BF16)
    by_expert = dot(gather, chosen)
    for k in range(ids.shape[0]):
        hit = ids[k : k + 1, :] == expert
        dcomb[k : k + 1, :] = jnp.sum(jnp.where(hit, by_expert, 0.0), axis=0, keepdims=True)

    for t in range(2):
        all_blocks(sent[t], got[t], t).wait_send()
        for j in range(last):
            for h in range(2):
                if j < last - 1 or h == 0:
                    to_right(t, j, h, mine).wait_send()
                if j < last - 1 or h == 1:
                    to_left(t, j, h, mine).wait_send()
        for i in range(nz):
            to_sib(t, i, mine).wait_send()
    all_blocks(sback, rback, 2).wait_send()
    comb_all.wait_send()
    for k in range(nz):
        pair(k).wait_send()
    for k in range(1, last + 1):
        for h in range(2):
            if k < last or h == 0:
                sum_right(k, h).wait_send()
            if k < last or h == 1:
                sum_left(k, h).wait_send()
    out.wait()


def per_device(n_ep, n_tp, tokens, grad_out, combine, expert_ids, w_gate, w_up, w_down):
    tok_count, feat = tokens.shape
    top = expert_ids.shape[1]
    hid, width = w_down.shape[1:]
    slots = n_ep * CAP
    nz = n_tp // 2
    vmem = pl.BlockSpec(memory_space=pltpu.VMEM)
    anyw = pl.BlockSpec(memory_space=pl.ANY)
    dma = pltpu.SemaphoreType.DMA
    blocks = pltpu.VMEM((n_ep, 16, 128), BF16)
    chunks = pltpu.VMEM((n_tp, slots, feat), BF16)
    parts = pltpu.VMEM((nz, slots, feat), BF16)
    d_tokens, d_combine, down = pl.pallas_call(
        functools.partial(kernel, n_ep, n_tp),
        out_shape=(
            jax.ShapeDtypeStruct((tok_count, feat), BF16),
            jax.ShapeDtypeStruct((top, tok_count), F32),
            jax.ShapeDtypeStruct((hid, width), BF16),
        ),
        in_specs=[vmem, vmem, vmem, vmem, anyw, anyw, anyw],
        out_specs=(vmem, vmem, anyw),
        scratch_shapes=[
            pltpu.VMEM((256, width), BF16),
            pltpu.VMEM((128, width), BF16),
            pltpu.VMEM((n_ep * 16, tok_count), BF16),
            pltpu.VMEM((n_ep * 16, tok_count), BF16),
            blocks,
            blocks,
            blocks,
            blocks,
            chunks,
            chunks,
            pltpu.VMEM((slots, 256), F32),
            pltpu.VMEM((slots, 128), F32),
            pltpu.VMEM((slots, 128), F32),
            pltpu.VMEM((slots, 256), BF16),
            pltpu.VMEM((slots, 128), BF16),
            pltpu.VMEM((n_tp, 8, 128), F32),
            parts,
            parts,
            parts,
            parts,
            pltpu.VMEM((nz // 2, slots, feat), BF16),
            pltpu.VMEM((nz // 2, slots, feat), BF16),
            blocks,
            blocks,
            pltpu.VMEM((hid, width), BF16),
            dma((3,)),
            dma((3,)),
            dma((3,)),
            dma((2, nz // 2, 2)),
            dma((2, nz // 2, 2)),
            dma((2, nz // 2, 2)),
            dma((2, nz // 2, 2)),
            dma((2, nz)),
            dma((2, nz)),
            dma((nz,)),
            dma((nz,)),
            dma((nz // 2, 2)),
            dma((nz // 2, 2)),
            dma((nz // 2, 2)),
            dma((nz // 2, 2)),
            dma,
            dma,
            dma,
        ],
        compiler_params=pltpu.CompilerParams(
            collective_id=0, has_side_effects=True, vmem_limit_bytes=48 * 1024 * 1024
        ),
    )(expert_ids.T, combine.T, tokens, grad_out, w_gate[0].T, w_up[0].T, w_down[0])
    return d_tokens, d_combine.T, down[None]


def solution(mesh):
    placed = (
        P("ep", "tp"),
        P("ep", "tp"),
        P("ep", None),
        P("ep", None),
        P("ep", None, "tp"),
        P("ep", None, "tp"),
        P("ep", "tp", None),
    )
    return jax.shard_map(
        functools.partial(per_device, mesh.shape["ep"], mesh.shape["tp"]),
        mesh=mesh,
        in_specs=placed,
        out_specs=(P("ep", "tp"), P("ep", None), P("ep", "tp", None)),
        check_vma=False,
    )
```

time: 266 us -> 105 us (0.39)
  blocking collectives: 103 us -> 0 us
  Pallas kernels: 0 us -> 95.9 us
  waiting for transfers between devices: 95.9 us -> 0 us
  starting transfers between devices: 19.4 us -> 0 us
  between operations: 14 us -> 0.66 us
  matrix products: 12.6 us -> 0 us
  local copies, waits for them, and re-layouts: 16.5 us -> 7.59 us
    pallas_call x0 -> x1, Pallas kernels: none -> 95.9 us  [per_device(): pl.pallas_call(functools.partial(kernel, n_ep, n_tp), out_shape=(jax.Shap...]
    all_gather x2 -> x0, waiting for transfers between devices: 77 us -> none  [the longest x1 50.1 us: per_device(): lax.all_gather(dy_recv, 'tp', axis=2, tiled=True)]
    all_to_all x3 -> x0, blocking collectives: 58.1 us -> none  [the longest x1 26.4 us: per_device(): lax.all_to_all(x_slots.reshape(expert_count, capacity, feat_local), 'ep',...]
    unnamed x1 -> x0, blocking collectives: 45.4 us -> none
    all_to_all x2 -> x0, starting transfers between devices: 19.3 us -> none  [the longest x1 12.4 us: per_device(): lax.all_to_all(comb_sum.astype(jnp.bfloat16), 'ep', split_axis=0, concat_...]
    all_to_all x2 -> x0, waiting for transfers between devices: 13.7 us -> none  [the longest x1 8.11 us: per_device(): lax.all_to_all(rounded.astype(jnp.bfloat16), 'ep', split_axis=0, concat_a...]
    dot_general x8 -> x0, matrix products: 12.6 us -> none  [the longest x1 3.29 us: per_device(): both_pre = jnp.dot(full_x, paired, preferred_element_type=jnp.float32)]
    reshape x4 -> x0, local copies, waits for them, and re-layouts: 6.96 us -> none  [the longest x1 3.41 us: per_device(): full_dy = full_dy.reshape(slot_total, -1)]
  transfers between devices with their start and end apart: 5 -> 0, of which waited for: 5 -> 0; matrix products, arithmetic and copies ran while one was open for 6% -> 0% of each run, Pallas kernels for 0% -> 0%
where the time goes in v1:
time: 105 us; the launch traced here: 104 us
  Pallas kernels  95.9 us (91%)
  local copies, waits for them, and re-layouts  7.59 us (7%)
    pallas_call x1, Pallas kernels, per_device(): pl.pallas_call(functools.partial(kernel, n_ep, n_tp), out_shape=(jax.Shap...  95.9 us
    unnamed x17, local copies, waits for them, and re-layouts  7.59 us

profile of v1, /device:TPU:1, one launch (start us, length us, event | category | flops | bytes accessed | tf_op | source)
XLA Modules:
  0.0 104.1 jit_solution(13736866706282853940)
XLA Ops:
  0.6 0.0 copy-start.5
  0.6 0.0 copy-start.6
  0.7 0.7 copy-done.5
  1.3 0.0 copy-done.6
  1.3 0.0 copy-start
  1.3 1.1 %copy-done = bf16[1,4096,96]{1,2,0:T(8,128)(2,1)S(1)} copy-done((bf16[1,4096,96]{1,2,0:T(8,128)(2,1)S(1)}, bf16[1,4096,96]{1,2,0:T(8,128)(2,1)}, u32[]{:S(2)}) %copy-start) | copy-done | bytes 786456
  2.5 0.0 copy-start.1
  2.5 1.1 %copy-done.1 = bf16[1,4096,96]{1,2,0:T(8,128)(2,1)S(1)} copy-done((bf16[1,4096,96]{1,2,0:T(8,128)(2,1)S(1)}, bf16[1,4096,96]{1,2,0:T(8,128)(2,1)}, u32[]{:S(2)}) %copy-start.1) | copy-done | bytes 786456
  3.6 0.0 copy-start.2
  3.6 1.1 %copy-done.2 = bf16[1,96,4096]{2,1,0:T(8,128)(2,1)S(1)} copy-done((bf16[1,96,4096]{2,1,0:T(8,128)(2,1)S(1)}, bf16[1,96,4096]{2,1,0:T(8,128)(2,1)}, u32[]{:S(2)}) %copy-start.2) | copy-done | bytes 786456
  4.7 0.0 copy-start.3
  4.7 0.7 copy-done.3
  5.5 0.0 copy-start.4
  5.5 0.7 copy-done.4
  6.2 95.9 %shard_map.94 = (bf16[32,256]{1,0:T(8,128)(2,1)S(1)}, f32[8,32]{1,0:T(8,128)S(1)}, bf16[96,4096]{1,0:T(8,128)(2,1)S(1)}) custom-call(s32[8,32]{1,0:T(8,128)S(1)} %bitcast.15, bf16[8,32]{1,0:T(8,128)(2,1)S(1)} %bitcast.17, bf16[32,256]{1,0:T(8,128)(2,1)S(1)} %copy-done.3, bf16[32,256]{1,0:T(8,128)(2,1)S(1)} %copy-done.4, bf16[96,4096]{1,0:T(8,128)(2,1)S(1)} %bitcast.12, ...), custom_call_target="tpu_custom_call" | custom-call | tf_op jit(solution)/shard_map/pallas_call | solution.py:465
  102.0 0.6 copy.13
  102.7 0.6 copy.14
  103.3 0.9 copy.15
Async XLA Ops:
  0.6 0.7 copy-start.5
  0.6 0.7 copy-start.6
  1.3 1.1 %copy-start = (bf16[1,4096,96]{1,2,0:T(8,128)(2,1)S(1)}, bf16[1,4096,96]{1,2,0:T(8,128)(2,1)}, u32[]{:S(2)}) copy-start(bf16[1,4096,96]{1,2,0:T(8,128)(2,1)} %param.11) | copy-start | bytes 2359300
  2.5 1.1 %copy-start.1 = (bf16[1,4096,96]{1,2,0:T(8,128)(2,1)S(1)}, bf16[1,4096,96]{1,2,0:T(8,128)(2,1)}, u32[]{:S(2)}) copy-start(bf16[1,4096,96]{1,2,0:T(8,128)(2,1)} %param.12) | copy-start | bytes 2359300
  3.6 1.1 %copy-start.2 = (bf16[1,96,4096]{2,1,0:T(8,128)(2,1)S(1)}, bf16[1,96,4096]{2,1,0:T(8,128)(2,1)}, u32[]{:S(2)}) copy-start(bf16[1,96,4096]{2,1,0:T(8,128)(2,1)} %param.13) | copy-start | bytes 2359300
  4.7 0.7 copy-start.3
  5.5 0.7 copy-start.4

commit v2 on v1

v2 whole, which is shorter than its diff:
```python
import functools
import math

import jax
import jax.numpy as jnp
from jax import lax
from jax.experimental import pallas as pl
from jax.experimental.pallas import tpu as pltpu
from jax.sharding import PartitionSpec as P

MESH = pl.DeviceIdType.MESH
F32 = jnp.float32
BF16 = jnp.bfloat16
CAP = 5
ROWS = 6
NN = (((1,), (0,)), ((), ()))
NT = (((1,), (1,)), ((), ()))
TN = (((0,), (0,)), ((), ()))


def dot(a, b, dims=NN, precision=None):
    return lax.dot_general(a, b, dims, preferred_element_type=F32, precision=precision)


def iota(shape, dim):
    return lax.broadcasted_iota(jnp.int32, shape, dim)


def where_block(u, swapped, side):
    return (u & (side - 1)) * side + lax.div(u, side) if swapped else u


def slot_of(i):
    s = (i * 3277) >> 14
    return s, i - s * CAP


def block_of(r):
    u = (r * 10923) >> 16
    return u, r - u * ROWS


def ones_where(mask):
    return jnp.where(mask, 1.0, 0.0).astype(BF16)


def kernel(
    n_ep,
    n_tp,
    ids,
    comb,
    tok_hbm,
    gout_hbm,
    wg,
    wu,
    wd,
    dtok,
    dcomb,
    gdown,
    tok,
    gout,
    far,
    w2,
    wdp,
    hot,
    code,
    picks,
    places,
    s1,
    r1,
    s2,
    r2,
    fx,
    fdy,
    acc,
    acch,
    wcol,
    bg,
    wt,
    cb,
    pown,
    pout,
    pin,
    sbuf,
    arr_r,
    arr_l,
    gd,
    w_sem,
    ep_s,
    ep_r,
    ag_rs,
    ag_rr,
    ag_ls,
    ag_lr,
    sib_s,
    sib_r,
    pair_s,
    pair_r,
    rs_rs,
    rs_rr,
    rs_ls,
    rs_lr,
    cb_s,
    cb_r,
    gd_sem,
    far_s,
    far_r,
):
    side = s1.shape[2]
    nz = n_tp // 2
    ep = lax.axis_index("ep")
    tp = lax.axis_index("tp")
    gx = lax.div(ep, side)
    gy = lax.rem(ep, side)
    z = lax.div(tp, 2)
    c = lax.rem(tp, 2)
    right = lax.rem(z + 1, nz) * 2 + c
    left = lax.rem(z + nz - 1, nz) * 2 + c
    sib = z * 2 + 1 - c
    opposite = lax.rem(z + nz // 2, nz) * 2 + c
    slots = fx.shape[1]
    feat = fx.shape[2]
    half_rows = slots // 2
    hid = wg.shape[0]
    lines = n_ep * ROWS

    def rcopy(src, dst, s, r, axis, to):
        return pltpu.make_async_remote_copy(
            src_ref=src, dst_ref=dst, send_sem=s, recv_sem=r, device_id={axis: to}, device_id_type=MESH
        )

    def neighbour(i, along_y):
        if along_y:
            return gx * side + lax.rem(gy + i, side)
        return lax.rem(gx + i, side) * side + gy

    loads = (
        pltpu.make_async_copy(tok_hbm, tok, w_sem.at[0]),
        pltpu.make_async_copy(gout_hbm, gout, w_sem.at[1]),
        pltpu.make_async_copy(wg, w2.at[pl.ds(0, hid)], w_sem.at[2]),
        pltpu.make_async_copy(wu, w2.at[pl.ds(128, hid)], w_sem.at[3]),
        pltpu.make_async_copy(wd, wdp.at[pl.ds(0, hid)], w_sem.at[4]),
    )
    for load in loads:
        load.start()

    barrier = pltpu.get_barrier_semaphore()

    def greet_y(i, _):
        pl.semaphore_signal(barrier, inc=1, device_id={"ep": neighbour(i, True)}, device_id_type=MESH)
        return 0

    def greet_x(i, _):
        pl.semaphore_signal(barrier, inc=1, device_id={"ep": neighbour(i, False)}, device_id_type=MESH)
        return 0

    def greet_tp(i, _):
        pl.semaphore_signal(barrier, inc=1, device_id={"tp": lax.rem(tp + i, n_tp)}, device_id_type=MESH)
        return 0

    lax.fori_loop(1, side, greet_y, 0)
    lax.fori_loop(1, side, greet_x, 0)
    lax.fori_loop(1, n_tp, greet_tp, 0)

    tokens = tok.shape[0]
    expert = iota((n_ep, tokens), 0)
    named = jnp.zeros((n_ep, tokens), F32)
    weight = jnp.zeros((n_ep, tokens), F32)
    for k in range(ids.shape[0]):
        hit = ids[k : k + 1, :] == expert
        named = jnp.where(hit, 1.0, named)
        weight = jnp.where(hit, comb[k : k + 1, :].astype(F32), weight)
    earlier = ones_where(iota((tokens, tokens), 0) < iota((tokens, tokens), 1))
    rank = dot(named.astype(BF16), earlier)
    code[...] = jnp.where(named > 0.5, rank, 99.0)
    lane = iota((n_ep, 128), 1)
    scalars = jnp.zeros((n_ep, 128), F32)
    for k in range(CAP):
        one = jnp.sum(jnp.where(code[...] == k, weight, 0.0), axis=1, keepdims=True)
        scalars = jnp.where(lane == k, one, scalars)
    block, line = block_of(iota((lines, n_ep), 0))
    _, line_t = block_of(iota((lines, tokens), 0))
    for h in range(2):
        spread = where_block(block, h == 0, side) == iota((lines, n_ep), 1)
        rows = dot(ones_where(spread), code[...].astype(BF16))
        hot[h] = ones_where(rows == line_t.astype(F32))
        if h == 0:
            extra = dot(ones_where(spread & (line == CAP)), scalars.astype(BF16))

    def lay(t, tokens_of, more):
        for h in range(2):
            laid = dot(hot[h], tokens_of[:, 128 * h : 128 * h + 128])
            if h == 0 and more is not None:
                laid = laid + more
            s1[t, h] = laid.astype(BF16).reshape(side, side * ROWS, 128)

    loads[0].wait()
    lay(0, tok, extra)

    pl.semaphore_wait(barrier, 2 * (side - 1) + n_tp - 1)

    out_of, into = (s1, s2), (r1, r2)

    def swap(t, h, phase):
        along_y = (h == 0) == (phase == 0)
        me = gy if along_y else gx
        src, dst = out_of[phase], into[phase]

        def one(i, _):
            to = lax.rem(me + i, side)
            rcopy(
                src.at[t, h, to],
                dst.at[t, h, me],
                ep_s.at[t, h, phase],
                ep_r.at[t, h, phase],
                "ep",
                neighbour(i, along_y),
            ).start()
            return 0

        lax.fori_loop(1, side, one, 0)
        dst[t, h, pl.ds(me, 1)] = src[t, h, pl.ds(me, 1)]

    def swapped(t, h, phase):
        some = pl.ds(0, side - 1)
        return rcopy(
            out_of[phase].at[t, h, some],
            into[phase].at[t, h, some],
            ep_s.at[t, h, phase],
            ep_r.at[t, h, phase],
            "ep",
            neighbour(1, (h == 0) == (phase == 0)),
        )

    def to_opposite(t):
        return rcopy((tok, gout)[t], far.at[t], far_s.at[t], far_r.at[t], "tp", opposite)

    swap(0, 0, 0)
    swap(0, 1, 0)
    loads[1].wait()
    lay(1, gout, None)
    swap(1, 0, 0)
    swap(1, 1, 0)
    to_opposite(0).start()
    to_opposite(1).start()

    gap = 128 - hid
    blank = jnp.zeros((gap, w2.shape[1]), BF16)
    w2[pl.ds(hid, gap), :] = blank
    w2[pl.ds(128 + hid, gap), :] = blank
    wdp[pl.ds(hid, gap), :] = blank
    acc[...] = jnp.zeros_like(acc)
    acch[...] = jnp.zeros_like(acch)
    block, line = block_of(iota((lines, lines), 0))
    turn = ones_where(where_block(block, True, side) * ROWS + line == iota((lines, lines), 1))

    source, slot = slot_of(iota((slots, lines), 0))
    column = iota((slots, lines), 1)
    picks[0] = ones_where(source * ROWS + slot == column)
    picks[1] = ones_where(where_block(source, True, side) * ROWS + slot == column)
    picks[2] = ones_where(source * ROWS + CAP == column)

    def forward(t, h):
        swapped(t, h, 0).wait_recv()
        turned = dot(turn, r1[t, h].reshape(lines, 128))
        s2[t, h] = turned.astype(BF16).reshape(side, side * ROWS, 128)
        swap(t, h, 1)

    for t in range(2):
        for h in range(2):
            forward(t, h)
    for load in loads[2:]:
        load.wait()

    full = (fx, fdy)
    last = nz // 2

    def half(ref, h):
        return ref.at[pl.ds(h * half_rows, half_rows)]

    def chunk(k, own):
        return lax.rem(z + k + nz, nz) * 2 + (c if own else 1 - c)

    def to_right(t, j, h, q):
        piece = half(full[t].at[q], h)
        return rcopy(piece, piece, ag_rs.at[t, j, h], ag_rr.at[t, j, h], "tp", right)

    def to_left(t, j, h, q):
        piece = half(full[t].at[q], h)
        return rcopy(piece, piece, ag_ls.at[t, j, h], ag_lr.at[t, j, h], "tp", left)

    def to_sib(t, i, q):
        piece = full[t].at[q]
        return rcopy(piece, piece, sib_s.at[t, i], sib_r.at[t, i], "tp", sib)

    def consume(t, q):
        columns = pl.ds(pl.multiple_of(q * feat, feat), feat)
        if t == 0:
            acc[...] += dot(fx[q], w2[:, columns], NT)
        else:
            acch[...] += dot(fdy[q], wdp[:, columns], NT)

    def consume_pair(t, j, own):
        def one(i, _):
            consume(t, chunk(j * (2 * i - 1), own))
            return 0

        lax.fori_loop(0, 2, one, 0)

    mine = chunk(0, True)

    def unpack(t, blocks, q):
        for h in range(2):
            swapped(blocks, h, 1).wait_recv()
            packed = dot(picks[h], r2[blocks, h].reshape(lines, 128))
            full[t][q, :, 128 * h : 128 * h + 128] = packed.astype(BF16)

    def own_chunk(t):
        unpack(t, t, mine)
        to_right(t, 0, 0, mine).start()
        to_left(t, 0, 1, mine).start()
        to_right(t, 0, 1, mine).start()
        to_left(t, 0, 0, mine).start()
        to_sib(t, 0, mine).start()
        consume(t, mine)

    def arrival(t, j):
        from_left, from_right = chunk(-j, True), chunk(j, True)
        for h in range(2):
            to_right(t, j - 1, h, from_left).wait_recv()
            if j < last - 1:
                to_right(t, j, h, from_left).start()
            to_left(t, j - 1, 1 - h, from_right).wait_recv()
            if j < last - 1:
                to_left(t, j, 1 - h, from_right).start()
        to_sib(t, j, from_left).start()
        to_sib(t, last + j, from_right).start()
        consume_pair(t, j, True)

    def from_sib(t, j):
        to_sib(t, j, chunk(-j, False)).wait_recv()
        if 0 < j < last:
            to_sib(t, last + j, chunk(j, False)).wait_recv()
            consume_pair(t, j, False)
        else:
            consume(t, chunk(j, False))

    def farthest(t):
        q = chunk(last, True)
        unpack(t, 3 + t, q)
        to_sib(t, last, q).start()
        consume(t, q)

    own_chunk(0)
    own_chunk(1)
    picked = dot(picks[2], r2[0, 0].reshape(lines, 128))
    _, slot_here = slot_of(iota((slots, 128), 0))
    picked = jnp.where(iota((slots, 128), 1) == slot_here, picked, 0.0).astype(BF16)
    wcol[...] = dot(picked, jnp.ones((128, 128), BF16))
    for t in range(2):
        to_opposite(t).wait_recv()
        lay(3 + t, far.at[t], None)
        swap(3 + t, 0, 0)
        swap(3 + t, 1, 0)
    for t in range(2):
        arrival(t, 1)
    for t in range(2):
        for h in range(2):
            forward(3 + t, h)
    for t in range(2):
        from_sib(t, 0)
        from_sib(t, 1)
    for t in range(2):
        arrival(t, 2)
    source, slot = slot_of(iota((lines, slots), 1))
    row = iota((lines, slots), 0)
    major = where_block(source, True, side) * ROWS
    places[0] = ones_where(row == major + slot)
    places[1] = ones_where(row == source * ROWS + slot)
    places[2] = ones_where(row == major + CAP)
    for t in range(2):
        farthest(t)
        from_sib(t, 2)
    for t in range(2):
        arrival(t, 3)
    for t in range(2):
        from_sib(t, last)
        from_sib(t, 3)

    for g in range(slots // 80):
        rows = pl.ds(80 * g, 80)
        gate, up, back = acc[rows, :128], acc[rows, 128:], acch[rows, :]
        w = wcol[rows, :]
        sigma = jax.nn.sigmoid(gate)
        act = gate * sigma
        product = act * up
        scaled = w * back
        bg[rows, :128] = (scaled * up * sigma * (1.0 + gate * (1.0 - sigma))).astype(BF16)
        bg[rows, 128:] = (scaled * act).astype(BF16)
        acch[rows, :] = product.astype(BF16).astype(F32) * back
        wcol[rows, :] = w * product

    def pair(k):
        return rcopy(pout.at[k], pin.at[k], pair_s.at[k], pair_r.at[k], "tp", sib)

    def calc(k):
        def part(q):
            columns = pl.ds(pl.multiple_of(q * feat, feat), feat)
            return dot(bg[...], w2[:, columns]).astype(BF16)

        pout[k] = part(chunk(k, False))
        pair(k).start()
        pown[k] = part(chunk(k, True))

    def calc_pair(k):
        def one(i, _):
            calc(k + i * (nz - 2 * k))
            return 0

        lax.fori_loop(0, 2, one, 0)

    def put(k, h, arrived):
        rows = pl.ds(h * half_rows, half_rows)
        value = pown[k, rows, :].astype(F32) + pin[k, rows, :].astype(F32)
        if arrived is not None:
            value = value + arrived[rows, :].astype(F32)
        sbuf[k, rows, :] = value.astype(BF16)

    def sum_right(k, h):
        return rcopy(
            half(sbuf.at[k], h), half(arr_r.at[k - 1], h), rs_rs.at[k - 1, h], rs_rr.at[k - 1, h], "tp", right
        )

    def sum_left(k, h):
        return rcopy(
            half(sbuf.at[nz - k], h), half(arr_l.at[k - 1], h), rs_ls.at[k - 1, h], rs_lr.at[k - 1, h], "tp", left
        )

    def tell(i, _):
        rcopy(cb.at[tp], cb.at[tp], cb_s, cb_r, "tp", lax.rem(tp + i, n_tp)).start()
        return 0

    calc(last)
    calc_pair(last - 1)
    cb[tp, :, :slots] = dot(jnp.ones((8, 128), F32), acch[...], NT, lax.Precision.HIGHEST)
    lax.fori_loop(1, n_tp, tell, 0)
    pair(last).wait_recv()
    put(last, 0, None)
    sum_right(last, 0).start()
    put(last, 1, None)
    sum_left(last, 1).start()
    for k in range(last - 1, 0, -1):
        first = k == last - 1
        pair(k).wait_recv()
        if not first:
            sum_right(k + 1, 1).wait_recv()
        put(k, 1, None if first else arr_r.at[k])
        sum_right(k, 1).start()
        pair(nz - k).wait_recv()
        if not first:
            sum_left(k + 1, 0).wait_recv()
        put(nz - k, 0, None if first else arr_l.at[k])
        sum_left(k, 0).start()
        if k > 1:
            calc_pair(k - 1)
        else:
            calc(0)
        sum_right(k + 1, 0).wait_recv()
        put(k, 0, arr_r.at[k])
        sum_right(k, 0).start()
        sum_left(k + 1, 1).wait_recv()
        put(nz - k, 1, arr_l.at[k])
        sum_left(k, 1).start()

    def down(q, _):
        columns = pl.ds(pl.multiple_of(q * feat, feat), feat)
        gd[:, columns] = dot(wt[...], fdy[q])[:hid].astype(BF16)
        return 0

    some = pl.ds(0, n_tp - 1)
    comb_all = rcopy(cb.at[some], cb.at[some], cb_s, cb_r, "tp", right)
    comb_all.wait_recv()
    comb_sum = jnp.sum(cb[...], axis=0)[:1, :slots]
    values = (places[2].astype(F32) * comb_sum).astype(BF16)
    _, slot_here = slot_of(iota((slots, 128), 0))
    extra = dot(values, ones_where(slot_here == iota((slots, 128), 1)))
    wt[...] = wcol[...].T.astype(BF16)
    pair(0).wait_recv()
    for h in (1, 0):
        sum_right(1, h).wait_recv()
        sum_left(1, h).wait_recv()
    total = pown[0].astype(F32) + pin[0].astype(F32) + arr_r[0].astype(F32) + arr_l[0].astype(F32)
    total = total.astype(BF16)
    for h in range(2):
        laid = dot(places[h], total[:, 128 * h : 128 * h + 128])
        if h == 0:
            laid = laid + extra
        s1[2, h] = laid.astype(BF16).reshape(side, side * ROWS, 128)
        swap(2, h, 0)
    lax.fori_loop(0, n_tp // 2, down, 0)
    for h in range(2):
        forward(2, h)
    lax.fori_loop(n_tp // 2, n_tp, down, 0)
    out = pltpu.make_async_copy(gd, gdown, gd_sem)
    out.start()

    for h in range(2):
        swapped(2, h, 1).wait_recv()
        back = r2[2, h].reshape(lines, 128)
        dtok[:, 128 * h : 128 * h + 128] = dot(hot[1 - h], back, TN).astype(BF16)
        if h == 0:
            column = iota((n_ep, lines), 1)
            told = dot(ones_where(iota((n_ep, lines), 0) * ROWS + CAP == column), back)
    by_expert = jnp.zeros((n_ep, tokens), F32)
    for k in range(CAP):
        by_expert = jnp.where(code[...] == k, told[:, k : k + 1], by_expert)
    for k in range(ids.shape[0]):
        hit = ids[k : k + 1, :] == expert
        dcomb[k : k + 1, :] = jnp.sum(jnp.where(hit, by_expert, 0.0), axis=0, keepdims=True)

    for t in range(5):
        for h in range(2):
            for phase in range(2):
                swapped(t, h, phase).wait_send()
    for t in range(2):
        to_opposite(t).wait_send()
        for j in range(last - 1):
            for h in range(2):
                to_right(t, j, h, mine).wait_send()
                to_left(t, j, h, mine).wait_send()
        for i in range(nz):
            to_sib(t, i, mine).wait_send()
    comb_all.wait_send()
    for k in range(nz):
        pair(k).wait_send()
    for k in range(1, last + 1):
        for h in range(2):
            if k < last or h == 0:
                sum_right(k, h).wait_send()
            if k < last or h == 1:
                sum_left(k, h).wait_send()
    out.wait()


def hand_over(tokens, combine, down, tokens_out, combine_out, down_out, a, b, c, in_sems, out_sems):
    part = down.shape[0] // 3
    moves = [(tokens, a, tokens_out), (combine, b, combine_out)]
    for i in range(3):
        rows = pl.ds(i * part, part)
        moves.append((down.at[rows], c.at[rows], down_out.at[rows]))
    inward = [pltpu.make_async_copy(x, y, in_sems.at[i]) for i, (x, y, _) in enumerate(moves)]
    outward = [pltpu.make_async_copy(y, z, out_sems.at[i]) for i, (_, y, z) in enumerate(moves)]
    for copy in inward:
        copy.start()
    for first, second in zip(inward, outward):
        first.wait()
        second.start()
    for copy in outward:
        copy.wait()


def per_device(n_ep, n_tp, tokens, grad_out, combine, expert_ids, w_gate, w_up, w_down):
    tok_count, feat = tokens.shape
    top = expert_ids.shape[1]
    hid, width = w_down.shape[1:]
    slots = n_ep * CAP
    nz = n_tp // 2
    side = math.isqrt(n_ep)
    vmem = pl.BlockSpec(memory_space=pltpu.VMEM)
    anyw = pl.BlockSpec(memory_space=pl.ANY)
    dma = pltpu.SemaphoreType.DMA
    blocks = pltpu.VMEM((5, 2, side, side * ROWS, 128), BF16)
    chunks = pltpu.VMEM((n_tp, slots, feat), BF16)
    parts = pltpu.VMEM((nz, slots, feat), BF16)
    results = pl.pallas_call(
        functools.partial(kernel, n_ep, n_tp),
        out_shape=(
            jax.ShapeDtypeStruct((tok_count, feat), BF16),
            jax.ShapeDtypeStruct((top, tok_count), F32),
            jax.ShapeDtypeStruct((hid, width), BF16),
        ),
        in_specs=[vmem] * 2 + [anyw] * 5,
        out_specs=(vmem, vmem, anyw),
        scratch_shapes=[
            pltpu.VMEM((tok_count, feat), BF16),
            pltpu.VMEM((tok_count, feat), BF16),
            pltpu.VMEM((2, tok_count, feat), BF16),
            pltpu.VMEM((256, width), BF16),
            pltpu.VMEM((128, width), BF16),
            pltpu.VMEM((2, n_ep * ROWS, tok_count), BF16),
            pltpu.VMEM((n_ep, tok_count), F32),
            pltpu.VMEM((3, slots, n_ep * ROWS), BF16),
            pltpu.VMEM((3, n_ep * ROWS, slots), BF16),
            blocks,
            blocks,
            blocks,
            blocks,
            chunks,
            chunks,
            pltpu.VMEM((slots, 256), F32),
            pltpu.VMEM((slots, 128), F32),
            pltpu.VMEM((slots, 128), F32),
            pltpu.VMEM((slots, 256), BF16),
            pltpu.VMEM((128, slots), BF16),
            pltpu.VMEM((n_tp, 8, 384), F32),
            parts,
            parts,
            parts,
            parts,
            pltpu.VMEM((nz // 2, slots, feat), BF16),
            pltpu.VMEM((nz // 2, slots, feat), BF16),
            pltpu.VMEM((hid, width), BF16),
            dma((5,)),
            dma((5, 2, 2)),
            dma((5, 2, 2)),
            dma((2, nz // 2 - 1, 2)),
            dma((2, nz // 2 - 1, 2)),
            dma((2, nz // 2 - 1, 2)),
            dma((2, nz // 2 - 1, 2)),
            dma((2, nz)),
            dma((2, nz)),
            dma((nz,)),
            dma((nz,)),
            dma((nz // 2, 2)),
            dma((nz // 2, 2)),
            dma((nz // 2, 2)),
            dma((nz // 2, 2)),
            dma,
            dma,
            dma,
            dma((2,)),
            dma((2,)),
        ],
        compiler_params=pltpu.CompilerParams(
            collective_id=0, has_side_effects=True, vmem_limit_bytes=60 * 1024 * 1024
        ),
    )(expert_ids.T, combine.T, tokens, grad_out, w_gate[0].T, w_up[0].T, w_down[0])
    d_tokens, d_combine, down = pl.pallas_call(
        hand_over,
        out_shape=tuple(jax.ShapeDtypeStruct(r.shape, r.dtype) for r in results),
        in_specs=[anyw] * 3,
        out_specs=(anyw,) * 3,
        scratch_shapes=[pltpu.VMEM(r.shape, r.dtype) for r in results] + [dma((5,)), dma((5,))],
        compiler_params=pltpu.CompilerParams(vmem_limit_bytes=60 * 1024 * 1024),
    )(*results)
    return d_tokens, d_combine.T, down[None]


def solution(mesh):
    placed = (
        P("ep", "tp"),
        P("ep", "tp"),
        P("ep", None),
        P("ep", None),
        P("ep", None, "tp"),
        P("ep", None, "tp"),
        P("ep", "tp", None),
    )
    return jax.shard_map(
        functools.partial(per_device, mesh.shape["ep"], mesh.shape["tp"]),
        mesh=mesh,
        in_specs=placed,
        out_specs=(P("ep", "tp"), P("ep", None), P("ep", "tp", None)),
        check_vma=False,
    )
```

time: 105 us -> 99.8 us (0.950)
  the two profiles are of different devices: /device:TPU:1 before, /device:TPU:2 now
where the time goes in v2:
time: 99.8 us; the launch traced here: 99.4 us
  Pallas kernels  98.8 us (99%)
    pallas_call x1, Pallas kernels, per_device(): pl.pallas_call(functools.partial(kernel, n_ep, n_tp), out_shape=(jax.Shap...  96.9 us

profile of v2, /device:TPU:2, one launch (start us, length us, event | category | flops | bytes accessed | tf_op | source)
XLA Modules:
  0.0 99.4 jit_solution(18116100728231107184)
XLA Ops:
  0.6 96.9 %shard_map.94 = (bf16[32,256]{1,0:T(8,128)(2,1)}, f32[8,32]{1,0:T(8,128)}, bf16[96,4096]{1,0:T(8,128)(2,1)}) custom-call(s32[8,32]{1,0:T(8,128)} %bitcast.14, bf16[8,32]{1,0:T(8,128)(2,1)} %bitcast.15, bf16[32,256]{1,0:T(8,128)(2,1)} %tok_hbm.1, bf16[32,256]{1,0:T(8,128)(2,1)} %gout_hbm.1, bf16[96,4096]{1,0:T(8,128)(2,1)} %bitcast.11, ...), custom_call_target="tpu_custom_call" | custom-call | tf_op jit(solution)/shard_map/pallas_call | solution.py:575
  97.5 1.9 %shard_map.95 = (bf16[32,256]{1,0:T(8,128)(2,1)}, f32[8,32]{1,0:T(8,128)}, bf16[96,4096]{1,0:T(8,128)(2,1)}) custom-call(bf16[32,256]{1,0:T(8,128)(2,1)} %get-tuple-element.9.tokens, f32[8,32]{1,0:T(8,128)} %get-tuple-element.10.combine, bf16[96,4096]{1,0:T(8,128)(2,1)} %get-tuple-element.11.down), custom_call_target="tpu_custom_call" | custom-call | tf_op jit(solution)/shard_map/pallas_call | solution.py:638

commit v3 on v2

--- a/solution.py
+++ b/solution.py
@@ -105,6 +105,8 @@
     gd_sem,
     far_s,
     far_r,
+    far_out,
+    far_in,
 ):
     side = s1.shape[2]
     nz = n_tp // 2
@@ -440,37 +442,47 @@
         rcopy(cb.at[tp], cb.at[tp], cb_s, cb_r, "tp", lax.rem(tp + i, n_tp)).start()
         return 0
 
+    def lay_sums(t, total, more):
+        for h in range(2):
+            laid = dot(places[h], total[:, 128 * h : 128 * h + 128])
+            if h == 0 and more is not None:
+                laid = laid + more
+            s1[t, h] = laid.astype(BF16).reshape(side, side * ROWS, 128)
+            swap(t, h, 0)
+
+    calc_pair(last - 1)
     calc(last)
-    calc_pair(last - 1)
-    cb[tp, :, :slots] = dot(jnp.ones((8, 128), F32), acch[...], NT, lax.Precision.HIGHEST)
-    lax.fori_loop(1, n_tp, tell, 0)
-    pair(last).wait_recv()
-    put(last, 0, None)
-    sum_right(last, 0).start()
-    put(last, 1, None)
-    sum_left(last, 1).start()
     for k in range(last - 1, 0, -1):
         first = k == last - 1
-        pair(k).wait_recv()
-        if not first:
-            sum_right(k + 1, 1).wait_recv()
-        put(k, 1, None if first else arr_r.at[k])
-        sum_right(k, 1).start()
-        pair(nz - k).wait_recv()
-        if not first:
-            sum_left(k + 1, 0).wait_recv()
-        put(nz - k, 0, None if first else arr_l.at[k])
-        sum_left(k, 0).start()
-        if k > 1:
+        for h in range(2):
+            if first and h == 0:
+                pair(k).wait_recv()
+            elif not first:
+                if h == 0:
+                    pair(k).wait_recv()
+                sum_right(k + 1, 1 - h).wait_recv()
+            put(k, 1 - h, None if first else arr_r.at[k])
+            sum_right(k, 1 - h).start()
+            if h == 0:
+                pair(nz - k).wait_recv()
+            if not first:
+                sum_left(k + 1, h).wait_recv()
+            put(nz - k, h, None if first else arr_l.at[k])
+            sum_left(k, h).start()
+            if h == 0 and not first:
+                if k > 1:
+                    calc_pair(k - 1)
+                else:
+                    calc(0)
+        if first:
+            cb[tp, :, :slots] = dot(jnp.ones((8, 128), F32), acch[...], NT, lax.Precision.HIGHEST)
+            lax.fori_loop(1, n_tp, tell, 0)
             calc_pair(k - 1)
-        else:
-            calc(0)
-        sum_right(k + 1, 0).wait_recv()
-        put(k, 0, arr_r.at[k])
-        sum_right(k, 0).start()
-        sum_left(k + 1, 1).wait_recv()
-        put(nz - k, 1, arr_l.at[k])
-        sum_left(k, 1).start()
+            pair(last).wait_recv()
+            lay_sums(5, (pown[last].astype(F32) + pin[last].astype(F32)).astype(BF16), None)
+        elif k == 2:
+            for h in range(2):
+                forward(5, h)
 
     def down(q, _):
         columns = pl.ds(pl.multiple_of(q * feat, feat), feat)
@@ -490,13 +502,12 @@
         sum_right(1, h).wait_recv()
         sum_left(1, h).wait_recv()
     total = pown[0].astype(F32) + pin[0].astype(F32) + arr_r[0].astype(F32) + arr_l[0].astype(F32)
-    total = total.astype(BF16)
+    lay_sums(2, total.astype(BF16), extra)
     for h in range(2):
-        laid = dot(places[h], total[:, 128 * h : 128 * h + 128])
-        if h == 0:
-            laid = laid + extra
-        s1[2, h] = laid.astype(BF16).reshape(side, side * ROWS, 128)
-        swap(2, h, 0)
+        swapped(5, h, 1).wait_recv()
+        far_out[:, 128 * h : 128 * h + 128] = dot(hot[1 - h], r2[5, h].reshape(lines, 128), TN)
+    cross = rcopy(far_out, far_in, far_s.at[2], far_r.at[2], "tp", opposite)
+    cross.start()
     lax.fori_loop(0, n_tp // 2, down, 0)
     for h in range(2):
         forward(2, h)
@@ -504,10 +515,12 @@
     out = pltpu.make_async_copy(gd, gdown, gd_sem)
     out.start()
 
+    cross.wait_recv()
     for h in range(2):
         swapped(2, h, 1).wait_recv()
         back = r2[2, h].reshape(lines, 128)
-        dtok[:, 128 * h : 128 * h + 128] = dot(hot[1 - h], back, TN).astype(BF16)
+        summed = dot(hot[1 - h], back, TN) + far_in[:, 128 * h : 128 * h + 128]
+        dtok[:, 128 * h : 128 * h + 128] = summed.astype(BF16)
         if h == 0:
             column = iota((n_ep, lines), 1)
             told = dot(ones_where(iota((n_ep, lines), 0) * ROWS + CAP == column), back)
@@ -518,7 +531,7 @@
         hit = ids[k : k + 1, :] == expert
         dcomb[k : k + 1, :] = jnp.sum(jnp.where(hit, by_expert, 0.0), axis=0, keepdims=True)
 
-    for t in range(5):
+    for t in range(6):
         for h in range(2):
             for phase in range(2):
                 swapped(t, h, phase).wait_send()
@@ -533,12 +546,11 @@
     comb_all.wait_send()
     for k in range(nz):
         pair(k).wait_send()
-    for k in range(1, last + 1):
-        for h in range(2):
-            if k < last or h == 0:
-                sum_right(k, h).wait_send()
-            if k < last or h == 1:
-                sum_left(k, h).wait_send()
+    for k in range(1, last):
+        for h in range(2):
+            sum_right(k, h).wait_send()
+            sum_left(k, h).wait_send()
+    cross.wait_send()
     out.wait()
 
 
@@ -569,7 +581,7 @@
     vmem = pl.BlockSpec(memory_space=pltpu.VMEM)
     anyw = pl.BlockSpec(memory_space=pl.ANY)
     dma = pltpu.SemaphoreType.DMA
-    blocks = pltpu.VMEM((5, 2, side, side * ROWS, 128), BF16)
+    blocks = pltpu.VMEM((6, 2, side, side * ROWS, 128), BF16)
     chunks = pltpu.VMEM((n_tp, slots, feat), BF16)
     parts = pltpu.VMEM((nz, slots, feat), BF16)
     results = pl.pallas_call(
@@ -611,8 +623,8 @@
             pltpu.VMEM((nz // 2, slots, feat), BF16),
             pltpu.VMEM((hid, width), BF16),
             dma((5,)),
-            dma((5, 2, 2)),
-            dma((5, 2, 2)),
+            dma((6, 2, 2)),
+            dma((6, 2, 2)),
             dma((2, nz // 2 - 1, 2)),
             dma((2, nz // 2 - 1, 2)),
             dma((2, nz // 2 - 1, 2)),
@@ -628,8 +640,10 @@
             dma,
             dma,
             dma,
-            dma((2,)),
-            dma((2,)),
+            dma((3,)),
+            dma((3,)),
+            pltpu.VMEM((tok_count, feat), F32),
+            pltpu.VMEM((tok_count, feat), F32),
         ],
         compiler_params=pltpu.CompilerParams(
             collective_id=0, has_side_effects=True, vmem_limit_bytes=60 * 1024 * 1024

time: 99.8 us -> 95.9 us (0.961)
  the two profiles are of different devices: /device:TPU:2 before, /device:TPU:1 now
where the time goes in v3:
time: 95.9 us; the launch traced here: 95.5 us
  Pallas kernels  94.9 us (99%)
    pallas_call x1, Pallas kernels, per_device(): pl.pallas_call(functools.partial(kernel, n_ep, n_tp), out_shape=(jax.Shap...  92.9 us
    pallas_call x1, Pallas kernels, per_device(): pl.pallas_call(hand_over, out_shape=tuple((jax.ShapeDtypeStruct(r.shape,...  1.93 us

profile of v3, /device:TPU:1, one launch (start us, length us, event | category | flops | bytes accessed | tf_op | source)
XLA Modules:
  0.0 95.5 jit_solution(16711750741796106238)
XLA Ops:
  0.6 92.9 %shard_map.94 = (bf16[32,256]{1,0:T(8,128)(2,1)}, f32[8,32]{1,0:T(8,128)}, bf16[96,4096]{1,0:T(8,128)(2,1)}) custom-call(s32[8,32]{1,0:T(8,128)} %bitcast.14, bf16[8,32]{1,0:T(8,128)(2,1)} %bitcast.15, bf16[32,256]{1,0:T(8,128)(2,1)} %tok_hbm.1, bf16[32,256]{1,0:T(8,128)(2,1)} %gout_hbm.1, bf16[96,4096]{1,0:T(8,128)(2,1)} %bitcast.11, ...), custom_call_target="tpu_custom_call" | custom-call | tf_op jit(solution)/shard_map/pallas_call | solution.py:587
  93.6 1.9 %shard_map.95 = (bf16[32,256]{1,0:T(8,128)(2,1)}, f32[8,32]{1,0:T(8,128)}, bf16[96,4096]{1,0:T(8,128)(2,1)}) custom-call(bf16[32,256]{1,0:T(8,128)(2,1)} %get-tuple-element.9.tokens, f32[8,32]{1,0:T(8,128)} %get-tuple-element.10.combine, bf16[96,4096]{1,0:T(8,128)(2,1)} %get-tuple-element.11.down), custom_call_target="tpu_custom_call" | custom-call | tf_op jit(solution)/shard_map/pallas_call | solution.py:652

commit v4 on v3

--- a/solution.py
+++ b/solution.py
@@ -475,9 +475,9 @@
                 else:
                     calc(0)
         if first:
+            calc_pair(k - 1)
             cb[tp, :, :slots] = dot(jnp.ones((8, 128), F32), acch[...], NT, lax.Precision.HIGHEST)
             lax.fori_loop(1, n_tp, tell, 0)
-            calc_pair(k - 1)
             pair(last).wait_recv()
             lay_sums(5, (pown[last].astype(F32) + pin[last].astype(F32)).astype(BF16), None)
         elif k == 2:

time: 95.9 us -> 95.7 us (level)
  no operation moved by 1% of the time
where the time goes in v4:
time: 95.7 us; the launch traced here: 95.3 us
  Pallas kernels  94.6 us (99%)
    pallas_call x1, Pallas kernels, per_device(): pl.pallas_call(functools.partial(kernel, n_ep, n_tp), out_shape=(jax.Shap...  92.7 us
    pallas_call x1, Pallas kernels, per_device(): pl.pallas_call(hand_over, out_shape=tuple((jax.ShapeDtypeStruct(r.shape,...  1.93 us

profile of v4, /device:TPU:1, one launch (start us, length us, event | category | flops | bytes accessed | tf_op | source)
XLA Modules:
  0.0 95.3 jit_solution(9297223941606109881)
XLA Ops:
  0.6 92.7 %shard_map.94 = (bf16[32,256]{1,0:T(8,128)(2,1)}, f32[8,32]{1,0:T(8,128)}, bf16[96,4096]{1,0:T(8,128)(2,1)}) custom-call(s32[8,32]{1,0:T(8,128)} %bitcast.14, bf16[8,32]{1,0:T(8,128)(2,1)} %bitcast.15, bf16[32,256]{1,0:T(8,128)(2,1)} %tok_hbm.1, bf16[32,256]{1,0:T(8,128)(2,1)} %gout_hbm.1, bf16[96,4096]{1,0:T(8,128)(2,1)} %bitcast.11, ...), custom_call_target="tpu_custom_call" | custom-call | tf_op jit(solution)/shard_map/pallas_call | solution.py:587
  93.4 1.9 %shard_map.95 = (bf16[32,256]{1,0:T(8,128)(2,1)}, f32[8,32]{1,0:T(8,128)}, bf16[96,4096]{1,0:T(8,128)(2,1)}) custom-call(bf16[32,256]{1,0:T(8,128)(2,1)} %get-tuple-element.9.tokens, f32[8,32]{1,0:T(8,128)} %get-tuple-element.10.combine, bf16[96,4096]{1,0:T(8,128)(2,1)} %get-tuple-element.11.down), custom_call_target="tpu_custom_call" | custom-call | tf_op jit(solution)/shard_map/pallas_call | solution.py:652
